TPU v7x, 256 devices: a whole 4x4x8 slice. The times are simulated.
256 devices in a mesh: cell: 32 (over z_lo, y, core), gene: 8 (over z_hi, x).
Axes of the slice: x: 4, y: 4, z: 8 (z_hi: 2, z_lo: 4; z = z_hi * 4 + z_lo), core: 2. Of those that a mesh axis runs over, the one named last changes fastest.
Arguments:
- counts: bfloat16 [65536, 16384], P('cell', 'gene'), may hold values from 0 to 25, as said below
- cell_factor: float32 [32, 65536], P(None, 'cell'), may hold values from 0.15 to 4.5, as said below
- gene_factor: float32 [32, 16384], P(None, 'gene'), may hold values from 0.15 to 4.5, as said below
Outputs:
- cell_result: float32 [32, 65536], P(None, 'cell')
- gene_result: float32 [32, 16384], P(None, 'gene')
Inputs may be any that keep to these rules, and one draw needn't show every extreme that they name: `counts`: whole numbers. `cell_factor`: positive. `gene_factor`: positive.
All inputs are finite; a program needn't handle non-finite values.
Results may differ from a plain program's by a relative error of at most 0.001.
Values sent between devices are 32-bit elements; how exact they have to be, the bound alone decides.
No kernel may reach another device: no remote copies, remote signals or barrier semaphores. Data moves between devices by JAX's collectives and lax.ppermute only.
A program may use at most 64 MiB of HBM per device.

v0:
```python
import functools

import jax
import jax.numpy as jnp
from jax import lax
from jax.experimental import pallas as pl
from jax.experimental.pallas import tpu as pltpu
from jax.sharding import Mesh
from jax.sharding import PartitionSpec as P

ITERS = 3
RANK = 32
GROUPS = 4
LANES = 128
WIDE = 1024
CORES, Y, X = 2, 4, 4
SMALL_VMEM, PASS_VMEM = 4 << 20, 28 << 20
F32, BF16 = jnp.float32, jnp.bfloat16

AT_CORE, AT_Y, AT_Z, AT_X = range(4)


def struct(shape, dtype=F32):
    return jax.ShapeDtypeStruct(shape, dtype)


def kernel_call(kernel, info, operands, out_shape, scratch=(), vmem=SMALL_VMEM, cost=None):
    return pl.pallas_call(
        kernel,
        grid_spec=pltpu.PrefetchScalarGridSpec(
            num_scalar_prefetch=1,
            grid=(),
            in_specs=[pl.BlockSpec(memory_space=pltpu.VMEM)] * len(operands),
            out_specs=jax.tree.map(lambda _: pl.BlockSpec(memory_space=pltpu.VMEM), out_shape),
            scratch_shapes=list(scratch),
        ),
        out_shape=out_shape,
        compiler_params=pltpu.CompilerParams(vmem_limit_bytes=vmem),
        cost_estimate=cost,
    )(info, *operands)


def pass_cost(cells, genes):
    return pl.CostEstimate(flops=cells, bytes_accessed=genes, transcendentals=0)


def ratio_of(counts, approx):
    return (counts.astype(F32) * pl.reciprocal(approx, approx=True)).astype(BF16)


def span(index, size):
    return pl.ds(pl.multiple_of(index * size, size), size)


def fill_genes(refs, side, groups):
    (ref,) = refs
    half = groups.shape[2]
    if ref.shape[0] == GROUPS:
        groups[...] = ref[:, :, span(side, half)]
        return
    width = ref.shape[2]
    n_z = half // width
    for y in range(Y):
        for z in range(n_z):
            groups[y, :, z * width : (z + 1) * width] = ref[y * n_z + z]


def gene_block(counts_ref, rows, cols, turned, copy, genes):
    approx = jnp.dot(turned, genes, preferred_element_type=F32)
    ratio = ratio_of(counts_ref[rows, cols], approx)
    return jnp.dot(copy, ratio, preferred_element_type=F32)


def gene_own(info, counts_ref, piece, gene_copy, out_ref):
    n_genes = counts_ref.shape[1]
    rows = span(info[AT_X], piece.shape[1])
    copy, turned = piece.astype(BF16), piece.T.astype(BF16)
    for start in range(0, n_genes, WIDE):
        cols = slice(start, start + WIDE)
        out_ref[:, cols] = gene_block(counts_ref, rows, cols, turned, copy, gene_copy[:, cols])


def gene_start_kernel(info, counts_ref, cells_ref, genes_ref, out_ref, gene_copy, *piece_refs):
    for s, ref in enumerate(piece_refs):
        ref[...] = cells_ref[:, span(lax.rem(info[AT_X] + (X - s), X), ref.shape[1])]
    gene_copy[...] = genes_ref[...].reshape(RANK, counts_ref.shape[1]).astype(BF16)
    gene_own(info, counts_ref, piece_refs[0][...], gene_copy, out_ref)


def gene_own_kernel(info, counts_ref, piece_ref, gene_copy, out_ref):
    gene_own(info, counts_ref, piece_ref[...], gene_copy, out_ref)


def gene_half(side, info, counts_ref, begun_ref, gene_copy, cell_copy, cell_turned, sums, out_ref):
    half = out_ref.shape[2] - LANES
    quarter = counts_ref.shape[0] // X
    cols = span(side, half)
    genes = gene_copy[:, cols]
    numer = begun_ref[:, cols]
    for s in range(1, X):
        rows = span(lax.rem(info[AT_X] + (X - s), X), quarter)
        part = slice(s * quarter, (s + 1) * quarter)
        numer = numer + gene_block(counts_ref, rows, cols, cell_turned[part, :], cell_copy[:, part], genes)
    out_ref[:, :, :half] = numer.reshape(GROUPS, 8, half)
    out_ref[:, :, half:] = sums[...].reshape(GROUPS, 8, LANES)


def gene_first_kernel(info, counts_ref, begun_ref, gene_copy, f0, f1, f2, f3, out_ref, cell_copy, cell_turned, sums):
    total = jnp.zeros((RANK, 1), F32)
    for s, ref in enumerate((f0, f1, f2, f3)):
        piece = ref[...]
        part = slice(s * piece.shape[1], (s + 1) * piece.shape[1])
        cell_copy[:, part] = piece.astype(BF16)
        cell_turned[part, :] = piece.T.astype(BF16)
        total = total + jnp.sum(piece, axis=1, keepdims=True)
    sums[...] = jnp.broadcast_to(total, (RANK, LANES))
    gene_half(1 - info[AT_CORE], info, counts_ref, begun_ref, gene_copy, cell_copy, cell_turned, sums, out_ref)


def gene_second_kernel(info, counts_ref, begun_ref, gene_copy, cell_copy, cell_turned, sums, out_ref):
    gene_half(info[AT_CORE], info, counts_ref, begun_ref, gene_copy, cell_copy, cell_turned, sums, out_ref)


def pass_call(kernel, info, operands, out_shape, cells, genes, scratch=()):
    return kernel_call(kernel, info, operands, out_shape, scratch, PASS_VMEM, pass_cost(cells, genes))


def gene_pass(info, counts, begun, gene_copy, cells):
    n_cells, n_genes = counts.shape
    half = n_genes // CORES
    out = struct((GROUPS, 8, half + LANES))
    made = [struct((RANK, n_cells), BF16), struct((n_cells, RANK), BF16), struct((RANK, LANES))]
    sent, *made = pass_call(gene_first_kernel, info, (counts, begun, gene_copy, *cells), [out] + made, n_cells, half)
    own = lambda: pass_call(gene_second_kernel, info, (counts, begun, gene_copy, *made), out, n_cells, half)
    return sent, made[1], own


def cell_block(to, info, counts_ref, cell_turned, gene_copy, sums, out_ref):
    n_genes = counts_ref.shape[1]
    quarter = out_ref.shape[1] - LANES
    rows = span(lax.rem(info[AT_X] + to, X), quarter)
    at = (X - to) % X * quarter
    out_ref[:, quarter:] = sums[...]
    cells = cell_turned[at : at + quarter, :]
    numer = jnp.zeros((RANK, quarter), F32)
    for start in range(0, n_genes, WIDE):
        cols = slice(start, start + WIDE)
        genes = gene_copy[:, cols]
        approx = jnp.dot(cells, genes, preferred_element_type=F32)
        ratio = ratio_of(counts_ref[rows, cols], approx)
        numer = numer + lax.dot_general(genes, ratio, (((1,), (1,)), ((), ())), preferred_element_type=F32)
    out_ref[:, :quarter] = numer


def cell_first_kernel(to, info, counts_ref, cell_turned, mine_ref, other_ref, out_ref, gene_copy, sums, ordered):
    half = ordered.shape[2] // CORES
    for side, ref in ((info[AT_CORE], mine_ref), (1 - info[AT_CORE], other_ref)):
        fill_genes([ref], side, ordered.at[:, :, span(side, half)])
    factor = ordered[...].reshape(RANK, CORES * half)
    gene_copy[...] = factor.astype(BF16)
    sums[...] = jnp.broadcast_to(jnp.sum(factor, axis=1, keepdims=True), (RANK, LANES))
    cell_block(to, info, counts_ref, cell_turned, gene_copy, sums, out_ref)


def cell_quarter(info, counts, to, cell_turned, left, first):
    n_cells, n_genes = counts.shape
    quarter = n_cells // X
    sums = struct((RANK, quarter + LANES))
    made = [struct((RANK, n_genes), BF16), struct((RANK, LANES))]
    return kernel_call(
        functools.partial(cell_first_kernel if first else cell_block, to),
        info,
        (counts, cell_turned, *left),
        [sums] + made if first else [sums],
        [pltpu.VMEM((GROUPS, 8, n_genes), F32)] if first else [],
        vmem=PASS_VMEM,
        cost=pass_cost(quarter, n_genes),
    )


def pair_sum_kernel(info, a_ref, b_ref, out_ref):
    width = out_ref.shape[2] - LANES
    half = a_ref.shape[2] - LANES
    n_z = half // width
    for y in range(Y):
        total = a_ref[y] + b_ref[y]
        for z in range(n_z):
            out_ref[y * n_z + z, :, :width] = total[:, z * width : (z + 1) * width]
            out_ref[y * n_z + z, :, width:] = total[:, half:]


def four_sum_kernel(info, a_ref, b_ref, c_ref, d_ref, out_ref):
    out_ref[...] = (a_ref[...] + b_ref[...]) + (c_ref[...] + d_ref[...])


def updated(piece, total):
    width = piece.shape[1]
    return piece * total[:, :width] / total[:, width : width + 1]


def gene_update_kernel(info, parts_ref, old_ref, new_ref, spread_ref):
    total = parts_ref[0]
    for i in range(1, parts_ref.shape[0]):
        total = total + parts_ref[i]
    width = new_ref.shape[1]
    if old_ref.ndim == 2:
        old = old_ref[...]
    else:
        n_z = parts_ref.shape[0] // Y
        old = old_ref[info[AT_Y], :, span(info[AT_CORE] * n_z + info[AT_Z], width)]
    new = updated(old, total)
    new_ref[...] = new
    for i in range(spread_ref.shape[0]):
        spread_ref[i] = new


def cell_update_kernel(info, old_ref, *refs):
    total = refs[0][...]
    for ref in refs[1:-1]:
        total = total + ref[...]
    refs[-1][...] = updated(old_ref[...], total)


def join_genes_kernel(info, mine_ref, other_ref, out_ref):
    half = out_ref.shape[2] // CORES
    for side, ref in ((info[AT_CORE], mine_ref), (1 - info[AT_CORE], other_ref)):
        fill_genes([ref], side, out_ref.at[:, :, span(side, half)])


def join_cells_kernel(info, *refs):
    for s, ref in enumerate(refs[:-1]):
        refs[-1][:, span(lax.rem(info[AT_X] + (X - s), X), ref.shape[1])] = ref[...]


def per_device(n_z, n_zhi, counts, cell_factor, gene_factor):
    n_cells, n_genes = counts.shape
    half, quarter, width = n_genes // CORES, n_cells // X, n_genes // (CORES * n_z)
    info = jnp.stack([lax.axis_index(a) for a in ("core", "y", "z", "x")]).astype(jnp.int32)
    swap = lambda a: lax.all_to_all(a, ("y", "z"), 0, 0, tiled=True)
    shift = lambda a, axis, n, s: lax.ppermute(a, axis, [(i, (i + s) % n) for i in range(n)])

    piece = gene_factor.reshape(GROUPS, 8, n_genes)
    begun, gene_copy, *cells = pass_call(
        gene_start_kernel,
        info,
        (counts, cell_factor, piece),
        [struct((RANK, n_genes)), struct((RANK, n_genes), BF16)] + [struct((RANK, quarter))] * X,
        quarter,
        n_genes,
    )
    for step in range(ITERS):
        if step:
            begun = pass_call(
                gene_own_kernel, info, (counts, cells[0], gene_copy), struct((RANK, n_genes)), quarter, n_genes
            )
        sent, cell_turned, own = gene_pass(info, counts, begun, gene_copy, cells)
        got = shift(sent, "core", CORES, 1)
        kept = own()
        parts = kernel_call(pair_sum_kernel, info, (kept, got), struct((Y * n_z, 8, width + LANES)))
        piece, spread = kernel_call(
            gene_update_kernel, info, (swap(parts), piece), [struct((8, width)), struct((Y * n_z, 8, width))]
        )
        mine = swap(spread)
        other = shift(mine, "core", CORES, 1)

        left = (mine, other)
        got = {}
        for s in (2, 1, 3, 0):
            sums, *made = cell_quarter(info, counts, s, cell_turned, left, not got)
            sums, left = lax.optimization_barrier((sums, made or left))
            got[s] = shift(sums, "x", X, s) if s else sums
        gene_copy = left[0]
        part = kernel_call(four_sum_kernel, info, [got[s] for s in range(X)], struct((RANK, quarter + LANES)))
        got = [shift(part, "z_hi", n_zhi, s) for s in range(1, n_zhi)]
        new = kernel_call(cell_update_kernel, info, (cells[0], part, *got), struct((RANK, quarter)))
        cells = [new] + [shift(new, "x", X, s) for s in (1, 2, 3)]
    joined = kernel_call(join_genes_kernel, info, (mine, other), struct((GROUPS, 8, n_genes)))
    cells = kernel_call(join_cells_kernel, info, cells, struct((RANK, n_cells)))
    return cells, joined.reshape(RANK, n_genes)


def solution(mesh):
    n_z, n_zhi = mesh.shape["cell"] // (Y * CORES), mesh.shape["gene"] // X
    cut = Mesh(mesh.devices.reshape(n_z, Y, CORES, n_zhi, X), ("z", "y", "core", "z_hi", "x"))
    cell, gene = ("z", "y", "core"), ("z_hi", "x")
    return jax.shard_map(
        functools.partial(per_device, n_z, n_zhi),
        mesh=cut,
        in_specs=(P(cell, gene), P(None, cell), P(None, gene)),
        out_specs=(P(None, cell), P(None, gene)),
        check_vma=False,
    )
```

profile of v0, /device:TPU:8, one launch (start us, length us, event | category | flops | bytes accessed | tf_op | source)
XLA Modules:
  0.0 216.5 jit_solution(329568057084221897)
XLA Ops:
  0.7 3.4 %copy-done = bf16[2048,2048]{1,0:T(8,128)(2,1)S(1)} copy-done((bf16[2048,2048]{1,0:T(8,128)(2,1)S(1)}, bf16[2048,2048]{1,0:T(8,128)(2,1)}, u32[]{:S(2)}) %copy-start) | copy-done | bytes 8388632
  4.1 0.9 copy-done.1
  5.0 0.9 copy-done.3
  6.0 1.6 shard_map.50
  7.6 2.2 %shard_map.51 = (f32[4,8,1152]{2,1,0:T(8,128)S(1)}, bf16[32,2048]{1,0:T(8,128)(2,1)S(1)}, bf16[2048,32]{1,0:T(8,128)(2,1)S(1)}, f32[32,128]{1,0:T(8,128)S(1)}) custom-call(s32[4]{0:T(128)S(1)} %pad_add_fusion.info, bf16[2048,2048]{1,0:T(8,128)(2,1)S(1)} %copy-done, f32[32,2048]{1,0:T(8,128)S(1)} %get-tuple-element.58.begun_ref, ...), custom_call_target="tpu_custom_call" | custom-call | flops 2048 | bytes 1024 | tf_op jit(solution)/shard_map/pallas_call | solution.py:28
  9.9 2.0 shard_map.52.a_ref
  12.5 16.8 %all_to_all.30.parts_ref = f32[16,8,384]{2,1,0:T(8,128)S(1)} all-to-all(f32[16,8,384]{2,1,0:T(8,128)S(1)} %shard_map.53), channel_id=1, replica_groups=mesh['z'=4,'y'=4,'core'=2,'z_hi'=2,'x'=4] {'y','z'}, dimensions={0} | all-to-all | bytes 393216 | tf_op jit(solution)/shard_map/all_to_all | solution.py:239
  29.3 0.6 shard_map.54
  30.0 12.1 %all_to_all.31.mine_ref = f32[16,8,256]{2,1,0:T(8,128)S(1)} all-to-all(f32[16,8,256]{2,1,0:T(8,128)S(1)} %get-tuple-element.67), channel_id=1, replica_groups=mesh['z'=4,'y'=4,'core'=2,'z_hi'=2,'x'=4] {'y','z'}, dimensions={0} | all-to-all | bytes 262144 | tf_op jit(solution)/shard_map/all_to_all | solution.py:239
  42.0 1.3 collective-permute-done.1.other_ref
  43.4 1.8 shard_map.55
  45.2 1.8 shard_map.56
  47.0 1.8 shard_map.57
  48.8 2.8 %collective-permute-start.4 = (f32[32,640]{1,0:T(8,128)S(1)}, f32[32,640]{1,0:T(8,128)S(1)}, u32[]{:S(2)}, u32[]{:S(2)}) collective-permute-start(f32[32,640]{1,0:T(8,128)S(1)} %shard_map.57), channel_id=1, source_target_pairs={{0,3},{1,0},{2,1},{3,2},{4,7},{5,4},{6,5},{7,6},{8,11},{9,8},{10,9... | collective-permute-start | bytes 245768 | tf_op jit(solution)/shard_map/ppermute | solution.py:240
  51.6 2.3 %collective-permute-start.3 = (f32[32,640]{1,0:T(8,128)S(1)}, f32[32,640]{1,0:T(8,128)S(1)}, u32[]{:S(2)}, u32[]{:S(2)}) collective-permute-start(f32[32,640]{1,0:T(8,128)S(1)} %get-tuple-element.76), channel_id=1, source_target_pairs={{0,2},{1,3},{2,0},{3,1},{4,6},{5,7},{6,4},{7,5},{8,10},{9,11},{10,... | collective-permute-start | bytes 245768 | tf_op jit(solution)/shard_map/ppermute | solution.py:240
  53.9 1.8 shard_map.58.a_ref
  55.6 3.1 %collective-permute-done.2.b_ref = f32[32,640]{1,0:T(8,128)S(1)} collective-permute-done((f32[32,640]{1,0:T(8,128)S(1)}, f32[32,640]{1,0:T(8,128)S(1)}, u32[]{:S(2)}, u32[]{:S(2)}) %collective-permute-start.2) | collective-permute-done | bytes 81952 | tf_op jit(solution)/shard_map/ppermute | solution.py:240
  59.3 4.6 %collective-permute-start.5 = (f32[32,640]{1,0:T(8,128)S(1)}, f32[32,640]{1,0:T(8,128)S(1)}, u32[]{:S(2)}, u32[]{:S(2)}) collective-permute-start(f32[32,640]{1,0:T(8,128)S(1)} %shard_map.59.refs_0_), channel_id=1, source_target_pairs={{0,4},{4,0},{1,5},{5,1},{2,6},{6,2},{3,7},{7,3},{8,12},{12,8},{9,1... | collective-permute-start | bytes 245768 | tf_op jit(solution)/shard_map/ppermute | solution.py:240
  63.9 4.6 %collective-permute-done.5.refs_1_ = f32[32,640]{1,0:T(8,128)S(1)} collective-permute-done((f32[32,640]{1,0:T(8,128)S(1)}, f32[32,640]{1,0:T(8,128)S(1)}, u32[]{:S(2)}, u32[]{:S(2)}) %collective-permute-start.5) | collective-permute-done | bytes 81952 | tf_op jit(solution)/shard_map/ppermute | solution.py:240
  69.2 1.8 collective-permute-start.8
  71.3 1.0 collective-permute-start.6
  72.2 1.6 shard_map.61.begun_ref
  73.9 3.3 %collective-permute-done.7.f2 = f32[32,512]{1,0:T(8,128)S(1)} collective-permute-done((f32[32,512]{1,0:T(8,128)S(1)}, f32[32,512]{1,0:T(8,128)S(1)}, u32[]{:S(2)}, u32[]{:S(2)}) %collective-permute-start.7) | collective-permute-done | bytes 65568 | tf_op jit(solution)/shard_map/ppermute | solution.py:240
  77.5 2.2 %shard_map.62 = (f32[4,8,1152]{2,1,0:T(8,128)S(1)}, bf16[32,2048]{1,0:T(8,128)(2,1)S(1)}, bf16[2048,32]{1,0:T(8,128)(2,1)S(1)}, f32[32,128]{1,0:T(8,128)S(1)}) custom-call(s32[4]{0:T(128)S(1)} %pad_add_fusion.info, bf16[2048,2048]{1,0:T(8,128)(2,1)S(1)} %copy-done, f32[32,2048]{1,0:T(8,128)S(1)} %shard_map.61.begun_ref, ...), custom_call_target="tpu_custom_call" | custom-call | flops 2048 | bytes 1024 | tf_op jit(solution)/shard_map/pallas_call | solution.py:28
  79.8 2.0 shard_map.63.a_ref
  82.4 12.0 %all_to_all.32.parts_ref = f32[16,8,384]{2,1,0:T(8,128)S(1)} all-to-all(f32[16,8,384]{2,1,0:T(8,128)S(1)} %shard_map.64), channel_id=1, replica_groups=mesh['z'=4,'y'=4,'core'=2,'z_hi'=2,'x'=4] {'y','z'}, dimensions={0} | all-to-all | bytes 393216 | tf_op jit(solution)/shard_map/all_to_all | solution.py:239
  94.3 0.6 shard_map.65
  95.0 12.3 %all_to_all.33.mine_ref = f32[16,8,256]{2,1,0:T(8,128)S(1)} all-to-all(f32[16,8,256]{2,1,0:T(8,128)S(1)} %get-tuple-element.84), channel_id=1, replica_groups=mesh['z'=4,'y'=4,'core'=2,'z_hi'=2,'x'=4] {'y','z'}, dimensions={0} | all-to-all | bytes 262144 | tf_op jit(solution)/shard_map/all_to_all | solution.py:239
  107.3 1.3 collective-permute-done.10.other_ref
  108.7 1.8 shard_map.66
  110.5 1.8 shard_map.67
  112.3 1.8 shard_map.68
  114.0 0.9 collective-permute-start.13
  115.0 1.1 collective-permute-start.11
  116.1 1.5 collective-permute-start.12
  117.6 1.8 shard_map.69.a_ref
  119.4 3.0 %collective-permute-done.11.b_ref = f32[32,640]{1,0:T(8,128)S(1)} collective-permute-done((f32[32,640]{1,0:T(8,128)S(1)}, f32[32,640]{1,0:T(8,128)S(1)}, u32[]{:S(2)}, u32[]{:S(2)}) %collective-permute-start.11) | collective-permute-done | bytes 81952 | tf_op jit(solution)/shard_map/ppermute | solution.py:240
  123.0 4.5 %collective-permute-start.14 = (f32[32,640]{1,0:T(8,128)S(1)}, f32[32,640]{1,0:T(8,128)S(1)}, u32[]{:S(2)}, u32[]{:S(2)}) collective-permute-start(f32[32,640]{1,0:T(8,128)S(1)} %shard_map.70.refs_0_), channel_id=1, source_target_pairs={{0,4},{4,0},{1,5},{5,1},{2,6},{6,2},{3,7},{7,3},{8,12},{12,8},{9,1... | collective-permute-start | bytes 245768 | tf_op jit(solution)/shard_map/ppermute | solution.py:240
  127.5 4.5 %collective-permute-done.14.refs_1_ = f32[32,640]{1,0:T(8,128)S(1)} collective-permute-done((f32[32,640]{1,0:T(8,128)S(1)}, f32[32,640]{1,0:T(8,128)S(1)}, u32[]{:S(2)}, u32[]{:S(2)}) %collective-permute-start.14) | collective-permute-done | bytes 81952 | tf_op jit(solution)/shard_map/ppermute | solution.py:240
  132.6 12.1 %collective-permute-start.17 = (f32[32,512]{1,0:T(8,128)S(1)}, f32[32,512]{1,0:T(8,128)S(1)}, u32[]{:S(2)}, u32[]{:S(2)}) collective-permute-start(f32[32,512]{1,0:T(8,128)S(1)} %shard_map.71.piece_ref.f0.old_ref), channel_id=1, source_target_pairs={{0,3},{1,0},{2,1},{3,2},{4,7},{5,4},{6,5},{7,6},{8,11},{9,8},{10,9... | collective-permute-start | bytes 196616 | tf_op jit(solution)/shard_map/ppermute | solution.py:240
  145.0 1.1 collective-permute-start.15
  146.1 1.6 shard_map.72.begun_ref
  147.8 2.8 %collective-permute-done.16.f2 = f32[32,512]{1,0:T(8,128)S(1)} collective-permute-done((f32[32,512]{1,0:T(8,128)S(1)}, f32[32,512]{1,0:T(8,128)S(1)}, u32[]{:S(2)}, u32[]{:S(2)}) %collective-permute-start.16) | collective-permute-done | bytes 65568 | tf_op jit(solution)/shard_map/ppermute | solution.py:240
  151.2 2.2 %shard_map.73 = (f32[4,8,1152]{2,1,0:T(8,128)S(1)}, bf16[32,2048]{1,0:T(8,128)(2,1)S(1)}, bf16[2048,32]{1,0:T(8,128)(2,1)S(1)}, f32[32,128]{1,0:T(8,128)S(1)}) custom-call(s32[4]{0:T(128)S(1)} %pad_add_fusion.info, bf16[2048,2048]{1,0:T(8,128)(2,1)S(1)} %copy-done, f32[32,2048]{1,0:T(8,128)S(1)} %shard_map.72.begun_ref, ...), custom_call_target="tpu_custom_call" | custom-call | flops 2048 | bytes 1024 | tf_op jit(solution)/shard_map/pallas_call | solution.py:28
  153.4 2.0 shard_map.74.a_ref
  156.0 12.2 %all_to_all.34.parts_ref = f32[16,8,384]{2,1,0:T(8,128)S(1)} all-to-all(f32[16,8,384]{2,1,0:T(8,128)S(1)} %shard_map.75), channel_id=1, replica_groups=mesh['z'=4,'y'=4,'core'=2,'z_hi'=2,'x'=4] {'y','z'}, dimensions={0} | all-to-all | bytes 393216 | tf_op jit(solution)/shard_map/all_to_all | solution.py:239
  168.2 1.2 shard_map.76
  169.5 12.1 %all_to_all.35.mine_ref = f32[16,8,256]{2,1,0:T(8,128)S(1)} all-to-all(f32[16,8,256]{2,1,0:T(8,128)S(1)} %get-tuple-element.101), channel_id=1, replica_groups=mesh['z'=4,'y'=4,'core'=2,'z_hi'=2,'x'=4] {'y','z'}, dimensions={0} | all-to-all | bytes 262144 | tf_op jit(solution)/shard_map/all_to_all | solution.py:239
  181.5 1.3 collective-permute-done.19.other_ref
  182.9 1.8 shard_map.77
  184.7 1.8 shard_map.78
  186.5 1.8 shard_map.79
  188.3 1.0 collective-permute-start.22
  189.3 1.0 collective-permute-start.20
  190.3 1.6 collective-permute-start.21
  191.9 1.8 shard_map.80.a_ref
  193.7 3.0 %collective-permute-done.20.b_ref = f32[32,640]{1,0:T(8,128)S(1)} collective-permute-done((f32[32,640]{1,0:T(8,128)S(1)}, f32[32,640]{1,0:T(8,128)S(1)}, u32[]{:S(2)}, u32[]{:S(2)}) %collective-permute-start.20) | collective-permute-done | bytes 81952 | tf_op jit(solution)/shard_map/ppermute | solution.py:240
  197.2 4.5 %collective-permute-start.23 = (f32[32,640]{1,0:T(8,128)S(1)}, f32[32,640]{1,0:T(8,128)S(1)}, u32[]{:S(2)}, u32[]{:S(2)}) collective-permute-start(f32[32,640]{1,0:T(8,128)S(1)} %shard_map.81.refs_0_), channel_id=1, source_target_pairs={{0,4},{4,0},{1,5},{5,1},{2,6},{6,2},{3,7},{7,3},{8,12},{12,8},{9,1... | collective-permute-start | bytes 245768 | tf_op jit(solution)/shard_map/ppermute | solution.py:240
  201.8 4.4 %collective-permute-done.23.refs_1_ = f32[32,640]{1,0:T(8,128)S(1)} collective-permute-done((f32[32,640]{1,0:T(8,128)S(1)}, f32[32,640]{1,0:T(8,128)S(1)}, u32[]{:S(2)}, u32[]{:S(2)}) %collective-permute-start.23) | collective-permute-done | bytes 81952 | tf_op jit(solution)/shard_map/ppermute | solution.py:240
  206.8 1.9 collective-permute-start.26
  208.8 1.2 collective-permute-start.24
  210.0 1.3 shard_map.84
  211.3 3.2 %collective-permute-done.25.refs_2_ = f32[32,512]{1,0:T(8,128)S(1)} collective-permute-done((f32[32,512]{1,0:T(8,128)S(1)}, f32[32,512]{1,0:T(8,128)S(1)}, u32[]{:S(2)}, u32[]{:S(2)}) %collective-permute-start.25) | collective-permute-done | bytes 65568 | tf_op jit(solution)/shard_map/ppermute | solution.py:240
  215.0 1.3 shard_map.83
  (40 shorter events, 7.9 us)
Async XLA Ops:
  0.7 3.4 %copy-start = (bf16[2048,2048]{1,0:T(8,128)(2,1)S(1)}, bf16[2048,2048]{1,0:T(8,128)(2,1)}, u32[]{:S(2)}) copy-start(bf16[2048,2048]{1,0:T(8,128)(2,1)} %counts_ref.41) | copy-start | bytes 25165828
  4.1 0.9 copy-start.1
  5.0 0.9 copy-start.3
  7.6 21.7 %copy-start.2 = (f32[32,2048]{1,0:T(8,128)S(1)}, f32[32,2048]{1,0:T(8,128)}, u32[]{:S(2)}) copy-start(f32[32,2048]{1,0:T(8,128)} %param.5) | copy-start | bytes 786436
  9.8 2.1 collective-permute-start
  42.0 1.3 collective-permute-start.1
  48.8 6.8 %collective-permute-start.4 = (f32[32,640]{1,0:T(8,128)S(1)}, f32[32,640]{1,0:T(8,128)S(1)}, u32[]{:S(2)}, u32[]{:S(2)}) collective-permute-start(f32[32,640]{1,0:T(8,128)S(1)} %shard_map.57), channel_id=1, source_target_pairs={{0,3},{1,0},{2,1},{3,2},{4,7},{5,4},{6,5},{7,6},{8,11},{9,8},{10,9... | collective-permute-start | bytes 245768 | tf_op jit(solution)/shard_map/ppermute | solution.py:240
  51.6 7.2 %collective-permute-start.2 = (f32[32,640]{1,0:T(8,128)S(1)}, f32[32,640]{1,0:T(8,128)S(1)}, u32[]{:S(2)}, u32[]{:S(2)}) collective-permute-start(f32[32,640]{1,0:T(8,128)S(1)} %shard_map.56), channel_id=1, source_target_pairs={{0,1},{1,2},{2,3},{3,0},{4,5},{5,6},{6,7},{7,4},{8,9},{9,10},{10,1... | collective-permute-start | bytes 245768 | tf_op jit(solution)/shard_map/ppermute | solution.py:240
  51.6 7.2 %collective-permute-start.3 = (f32[32,640]{1,0:T(8,128)S(1)}, f32[32,640]{1,0:T(8,128)S(1)}, u32[]{:S(2)}, u32[]{:S(2)}) collective-permute-start(f32[32,640]{1,0:T(8,128)S(1)} %get-tuple-element.76), channel_id=1, source_target_pairs={{0,2},{1,3},{2,0},{3,1},{4,6},{5,7},{6,4},{7,5},{8,10},{9,11},{10,... | collective-permute-start | bytes 245768 | tf_op jit(solution)/shard_map/ppermute | solution.py:240
  59.3 9.2 %collective-permute-start.5 = (f32[32,640]{1,0:T(8,128)S(1)}, f32[32,640]{1,0:T(8,128)S(1)}, u32[]{:S(2)}, u32[]{:S(2)}) collective-permute-start(f32[32,640]{1,0:T(8,128)S(1)} %shard_map.59.refs_0_), channel_id=1, source_target_pairs={{0,4},{4,0},{1,5},{5,1},{2,6},{6,2},{3,7},{7,3},{8,12},{12,8},{9,1... | collective-permute-start | bytes 245768 | tf_op jit(solution)/shard_map/ppermute | solution.py:240
  69.2 4.7 %collective-permute-start.8 = (f32[32,512]{1,0:T(8,128)S(1)}, f32[32,512]{1,0:T(8,128)S(1)}, u32[]{:S(2)}, u32[]{:S(2)}) collective-permute-start(f32[32,512]{1,0:T(8,128)S(1)} %shard_map.60.piece_ref.f0.old_ref), channel_id=1, source_target_pairs={{0,3},{1,0},{2,1},{3,2},{4,7},{5,4},{6,5},{7,6},{8,11},{9,8},{10,9... | collective-permute-start | bytes 196616 | tf_op jit(solution)/shard_map/ppermute | solution.py:240
  71.0 6.1 %collective-permute-start.7 = (f32[32,512]{1,0:T(8,128)S(1)}, f32[32,512]{1,0:T(8,128)S(1)}, u32[]{:S(2)}, u32[]{:S(2)}) collective-permute-start(f32[32,512]{1,0:T(8,128)S(1)} %shard_map.60.piece_ref.f0.old_ref), channel_id=1, source_target_pairs={{0,2},{1,3},{2,0},{3,1},{4,6},{5,7},{6,4},{7,5},{8,10},{9,11},{10,... | collective-permute-start | bytes 196616 | tf_op jit(solution)/shard_map/ppermute | solution.py:240
  71.3 6.3 %collective-permute-start.6 = (f32[32,512]{1,0:T(8,128)S(1)}, f32[32,512]{1,0:T(8,128)S(1)}, u32[]{:S(2)}, u32[]{:S(2)}) collective-permute-start(f32[32,512]{1,0:T(8,128)S(1)} %shard_map.60.piece_ref.f0.old_ref), channel_id=1, source_target_pairs={{0,1},{1,2},{2,3},{3,0},{4,5},{5,6},{6,7},{7,4},{8,9},{9,10},{10,1... | collective-permute-start | bytes 196616 | tf_op jit(solution)/shard_map/ppermute | solution.py:240
  79.7 2.1 collective-permute-start.9
  107.3 1.3 collective-permute-start.10
  114.0 5.4 %collective-permute-start.13 = (f32[32,640]{1,0:T(8,128)S(1)}, f32[32,640]{1,0:T(8,128)S(1)}, u32[]{:S(2)}, u32[]{:S(2)}) collective-permute-start(f32[32,640]{1,0:T(8,128)S(1)} %shard_map.68), channel_id=1, source_target_pairs={{0,3},{1,0},{2,1},{3,2},{4,7},{5,4},{6,5},{7,6},{8,11},{9,8},{10,9... | collective-permute-start | bytes 245768 | tf_op jit(solution)/shard_map/ppermute | solution.py:240
  115.0 7.4 %collective-permute-start.11 = (f32[32,640]{1,0:T(8,128)S(1)}, f32[32,640]{1,0:T(8,128)S(1)}, u32[]{:S(2)}, u32[]{:S(2)}) collective-permute-start(f32[32,640]{1,0:T(8,128)S(1)} %shard_map.67), channel_id=1, source_target_pairs={{0,1},{1,2},{2,3},{3,0},{4,5},{5,6},{6,7},{7,4},{8,9},{9,10},{10,1... | collective-permute-start | bytes 245768 | tf_op jit(solution)/shard_map/ppermute | solution.py:240
  116.1 6.3 %collective-permute-start.12 = (f32[32,640]{1,0:T(8,128)S(1)}, f32[32,640]{1,0:T(8,128)S(1)}, u32[]{:S(2)}, u32[]{:S(2)}) collective-permute-start(f32[32,640]{1,0:T(8,128)S(1)} %get-tuple-element.93), channel_id=1, source_target_pairs={{0,2},{1,3},{2,0},{3,1},{4,6},{5,7},{6,4},{7,5},{8,10},{9,11},{10,... | collective-permute-start | bytes 245768 | tf_op jit(solution)/shard_map/ppermute | solution.py:240
  123.0 9.0 %collective-permute-start.14 = (f32[32,640]{1,0:T(8,128)S(1)}, f32[32,640]{1,0:T(8,128)S(1)}, u32[]{:S(2)}, u32[]{:S(2)}) collective-permute-start(f32[32,640]{1,0:T(8,128)S(1)} %shard_map.70.refs_0_), channel_id=1, source_target_pairs={{0,4},{4,0},{1,5},{5,1},{2,6},{6,2},{3,7},{7,3},{8,12},{12,8},{9,1... | collective-permute-start | bytes 245768 | tf_op jit(solution)/shard_map/ppermute | solution.py:240
  132.6 15.1 %collective-permute-start.17 = (f32[32,512]{1,0:T(8,128)S(1)}, f32[32,512]{1,0:T(8,128)S(1)}, u32[]{:S(2)}, u32[]{:S(2)}) collective-permute-start(f32[32,512]{1,0:T(8,128)S(1)} %shard_map.71.piece_ref.f0.old_ref), channel_id=1, source_target_pairs={{0,3},{1,0},{2,1},{3,2},{4,7},{5,4},{6,5},{7,6},{8,11},{9,8},{10,9... | collective-permute-start | bytes 196616 | tf_op jit(solution)/shard_map/ppermute | solution.py:240
  144.7 5.8 %collective-permute-start.16 = (f32[32,512]{1,0:T(8,128)S(1)}, f32[32,512]{1,0:T(8,128)S(1)}, u32[]{:S(2)}, u32[]{:S(2)}) collective-permute-start(f32[32,512]{1,0:T(8,128)S(1)} %shard_map.71.piece_ref.f0.old_ref), channel_id=1, source_target_pairs={{0,2},{1,3},{2,0},{3,1},{4,6},{5,7},{6,4},{7,5},{8,10},{9,11},{10,... | collective-permute-start | bytes 196616 | tf_op jit(solution)/shard_map/ppermute | solution.py:240
  145.0 6.1 %collective-permute-start.15 = (f32[32,512]{1,0:T(8,128)S(1)}, f32[32,512]{1,0:T(8,128)S(1)}, u32[]{:S(2)}, u32[]{:S(2)}) collective-permute-start(f32[32,512]{1,0:T(8,128)S(1)} %shard_map.71.piece_ref.f0.old_ref), channel_id=1, source_target_pairs={{0,1},{1,2},{2,3},{3,0},{4,5},{5,6},{6,7},{7,4},{8,9},{9,10},{10,1... | collective-permute-start | bytes 196616 | tf_op jit(solution)/shard_map/ppermute | solution.py:240
  153.3 2.1 collective-permute-start.18
  181.5 1.3 collective-permute-start.19
  188.3 5.4 %collective-permute-start.22 = (f32[32,640]{1,0:T(8,128)S(1)}, f32[32,640]{1,0:T(8,128)S(1)}, u32[]{:S(2)}, u32[]{:S(2)}) collective-permute-start(f32[32,640]{1,0:T(8,128)S(1)} %shard_map.79), channel_id=1, source_target_pairs={{0,3},{1,0},{2,1},{3,2},{4,7},{5,4},{6,5},{7,6},{8,11},{9,8},{10,9... | collective-permute-start | bytes 245768 | tf_op jit(solution)/shard_map/ppermute | solution.py:240
  189.3 7.4 %collective-permute-start.20 = (f32[32,640]{1,0:T(8,128)S(1)}, f32[32,640]{1,0:T(8,128)S(1)}, u32[]{:S(2)}, u32[]{:S(2)}) collective-permute-start(f32[32,640]{1,0:T(8,128)S(1)} %shard_map.78), channel_id=1, source_target_pairs={{0,1},{1,2},{2,3},{3,0},{4,5},{5,6},{6,7},{7,4},{8,9},{9,10},{10,1... | collective-permute-start | bytes 245768 | tf_op jit(solution)/shard_map/ppermute | solution.py:240
  190.3 6.3 %collective-permute-start.21 = (f32[32,640]{1,0:T(8,128)S(1)}, f32[32,640]{1,0:T(8,128)S(1)}, u32[]{:S(2)}, u32[]{:S(2)}) collective-permute-start(f32[32,640]{1,0:T(8,128)S(1)} %get-tuple-element.110), channel_id=1, source_target_pairs={{0,2},{1,3},{2,0},{3,1},{4,6},{5,7},{6,4},{7,5},{8,10},{9,11},{10,... | collective-permute-start | bytes 245768 | tf_op jit(solution)/shard_map/ppermute | solution.py:240
  197.2 8.9 %collective-permute-start.23 = (f32[32,640]{1,0:T(8,128)S(1)}, f32[32,640]{1,0:T(8,128)S(1)}, u32[]{:S(2)}, u32[]{:S(2)}) collective-permute-start(f32[32,640]{1,0:T(8,128)S(1)} %shard_map.81.refs_0_), channel_id=1, source_target_pairs={{0,4},{4,0},{1,5},{5,1},{2,6},{6,2},{3,7},{7,3},{8,12},{12,8},{9,1... | collective-permute-start | bytes 245768 | tf_op jit(solution)/shard_map/ppermute | solution.py:240
  206.8 4.5 %collective-permute-start.26 = (f32[32,512]{1,0:T(8,128)S(1)}, f32[32,512]{1,0:T(8,128)S(1)}, u32[]{:S(2)}, u32[]{:S(2)}) collective-permute-start(f32[32,512]{1,0:T(8,128)S(1)} %shard_map.82.refs_0_), channel_id=1, source_target_pairs={{0,3},{1,0},{2,1},{3,2},{4,7},{5,4},{6,5},{7,6},{8,11},{9,8},{10,9... | collective-permute-start | bytes 196616 | tf_op jit(solution)/shard_map/ppermute | solution.py:240
  208.6 5.9 %collective-permute-start.25 = (f32[32,512]{1,0:T(8,128)S(1)}, f32[32,512]{1,0:T(8,128)S(1)}, u32[]{:S(2)}, u32[]{:S(2)}) collective-permute-start(f32[32,512]{1,0:T(8,128)S(1)} %shard_map.82.refs_0_), channel_id=1, source_target_pairs={{0,2},{1,3},{2,0},{3,1},{4,6},{5,7},{6,4},{7,5},{8,10},{9,11},{10,... | collective-permute-start | bytes 196616 | tf_op jit(solution)/shard_map/ppermute | solution.py:240
  208.8 6.2 %collective-permute-start.24 = (f32[32,512]{1,0:T(8,128)S(1)}, f32[32,512]{1,0:T(8,128)S(1)}, u32[]{:S(2)}, u32[]{:S(2)}) collective-permute-start(f32[32,512]{1,0:T(8,128)S(1)} %shard_map.82.refs_0_), channel_id=1, source_target_pairs={{0,1},{1,2},{2,3},{3,0},{4,5},{5,6},{6,7},{7,4},{8,9},{9,10},{10,1... | collective-permute-start | bytes 196616 | tf_op jit(solution)/shard_map/ppermute | solution.py:240
where the time goes:
time: 220 us; the launch traced here: 216 us
  blocking collectives  77.5 us (35%)
  Pallas kernels  49.2 us (22%)
  starting transfers between devices  45.9 us (21%)
  waiting for transfers between devices  37.5 us (17%)
  local copies, waits for them, and re-layouts  5.29 us (2%)
    all_to_all x6, blocking collectives, per_device(): swap = lambda a: lax.all_to_all(a, ('y', 'z'), 0, 0, tiled=True)  77.5 us
    pallas_call x35, Pallas kernels, kernel_call(): pl.pallas_call(kernel, grid_spec=pltpu.PrefetchScalarGridSpec(num_scalar_...  49.2 us
    ppermute x27, starting transfers between devices, per_device(): lax.ppermute(a, axis, [(i, (i + s) % n) for i in range(n)])  45.9 us
    ppermute x27, waiting for transfers between devices, per_device(): lax.ppermute(a, axis, [(i, (i + s) % n) for i in range(n)])  37.5 us
    unnamed x8, local copies, waits for them, and re-layouts  5.29 us
  transfers between devices with their start and end apart: 27, of which 15 were waited for; matrix products, arithmetic and copies ran while one was open for 0% of the time, Pallas kernels for 7%

commit v1 on v0

--- a/solution.py
+++ b/solution.py
@@ -71,24 +71,29 @@
     return jnp.dot(copy, ratio, preferred_element_type=F32)
 
 
-def gene_own(info, counts_ref, piece, gene_copy, out_ref):
+def gene_quarter(s, info, counts_ref, piece, gene_copy, out_ref, begun_ref=None):
     n_genes = counts_ref.shape[1]
-    rows = span(info[AT_X], piece.shape[1])
+    rows = span(lax.rem(info[AT_X] + (X - s), X), piece.shape[1])
     copy, turned = piece.astype(BF16), piece.T.astype(BF16)
     for start in range(0, n_genes, WIDE):
         cols = slice(start, start + WIDE)
-        out_ref[:, cols] = gene_block(counts_ref, rows, cols, turned, copy, gene_copy[:, cols])
+        numer = gene_block(counts_ref, rows, cols, turned, copy, gene_copy[:, cols])
+        out_ref[:, cols] = numer if begun_ref is None else begun_ref[:, cols] + numer
 
 
 def gene_start_kernel(info, counts_ref, cells_ref, genes_ref, out_ref, gene_copy, *piece_refs):
     for s, ref in enumerate(piece_refs):
         ref[...] = cells_ref[:, span(lax.rem(info[AT_X] + (X - s), X), ref.shape[1])]
     gene_copy[...] = genes_ref[...].reshape(RANK, counts_ref.shape[1]).astype(BF16)
-    gene_own(info, counts_ref, piece_refs[0][...], gene_copy, out_ref)
+    gene_quarter(0, info, counts_ref, piece_refs[0][...], gene_copy, out_ref)
 
 
 def gene_own_kernel(info, counts_ref, piece_ref, gene_copy, out_ref):
-    gene_own(info, counts_ref, piece_ref[...], gene_copy, out_ref)
+    gene_quarter(0, info, counts_ref, piece_ref[...], gene_copy, out_ref)
+
+
+def gene_next_kernel(info, counts_ref, piece_ref, gene_copy, begun_ref, out_ref):
+    gene_quarter(X - 1, info, counts_ref, piece_ref[...], gene_copy, out_ref, begun_ref)
 
 
 def gene_half(side, info, counts_ref, begun_ref, gene_copy, cell_copy, cell_turned, sums, out_ref):
@@ -97,7 +102,7 @@
     cols = span(side, half)
     genes = gene_copy[:, cols]
     numer = begun_ref[:, cols]
-    for s in range(1, X):
+    for s in range(1, X - 1):
         rows = span(lax.rem(info[AT_X] + (X - s), X), quarter)
         part = slice(s * quarter, (s + 1) * quarter)
         numer = numer + gene_block(counts_ref, rows, cols, cell_turned[part, :], cell_copy[:, part], genes)
@@ -135,31 +140,63 @@
     return sent, made[1], own
 
 
-def cell_block(to, info, counts_ref, cell_turned, gene_copy, sums, out_ref):
-    n_genes = counts_ref.shape[1]
-    quarter = out_ref.shape[1] - LANES
-    rows = span(lax.rem(info[AT_X] + to, X), quarter)
+def cell_rows(to, info, cell_turned, quarter):
     at = (X - to) % X * quarter
-    out_ref[:, quarter:] = sums[...]
-    cells = cell_turned[at : at + quarter, :]
-    numer = jnp.zeros((RANK, quarter), F32)
-    for start in range(0, n_genes, WIDE):
-        cols = slice(start, start + WIDE)
-        genes = gene_copy[:, cols]
-        approx = jnp.dot(cells, genes, preferred_element_type=F32)
-        ratio = ratio_of(counts_ref[rows, cols], approx)
-        numer = numer + lax.dot_general(genes, ratio, (((1,), (1,)), ((), ())), preferred_element_type=F32)
-    out_ref[:, :quarter] = numer
-
-
-def cell_first_kernel(to, info, counts_ref, cell_turned, mine_ref, other_ref, out_ref, gene_copy, sums, ordered):
+    return span(lax.rem(info[AT_X] + to, X), quarter), cell_turned[at : at + quarter, :]
+
+
+def cell_block(counts_ref, rows, cols, cells, genes):
+    approx = jnp.dot(cells, genes, preferred_element_type=F32)
+    ratio = ratio_of(counts_ref[rows, cols], approx)
+    return lax.dot_general(genes, ratio, (((1,), (1,)), ((), ())), preferred_element_type=F32)
+
+
+def cell_begin_kernel(to, info, counts_ref, cell_turned, mine_ref, out_ref, groups):
+    quarter, half = out_ref.shape[1], groups.shape[2]
+    fill_genes([mine_ref], 0, groups)
+    genes = groups[...].reshape(RANK, half).astype(BF16)
+    rows, cells = cell_rows(to, info, cell_turned, quarter)
+    out_ref[...] = cell_block(counts_ref, rows, span(info[AT_CORE], half), cells, genes)
+
+
+def cell_first_kernel(
+    to, info, counts_ref, cell_turned, begun_ref, mine_ref, other_ref, out_ref, gene_copy, sums, ordered
+):
     half = ordered.shape[2] // CORES
+    quarter = begun_ref.shape[1]
     for side, ref in ((info[AT_CORE], mine_ref), (1 - info[AT_CORE], other_ref)):
         fill_genes([ref], side, ordered.at[:, :, span(side, half)])
     factor = ordered[...].reshape(RANK, CORES * half)
     gene_copy[...] = factor.astype(BF16)
     sums[...] = jnp.broadcast_to(jnp.sum(factor, axis=1, keepdims=True), (RANK, LANES))
-    cell_block(to, info, counts_ref, cell_turned, gene_copy, sums, out_ref)
+    rows, cells = cell_rows(to, info, cell_turned, quarter)
+    cols = span(1 - info[AT_CORE], half)
+    out_ref[:, :quarter] = begun_ref[...] + cell_block(counts_ref, rows, cols, cells, gene_copy[:, cols])
+    out_ref[:, quarter:] = sums[...]
+
+
+def cell_later_kernel(to, info, counts_ref, cell_turned, gene_copy, sums, out_ref):
+    quarter = out_ref.shape[1] - LANES
+    rows, cells = cell_rows(to, info, cell_turned, quarter)
+    numer = jnp.zeros((RANK, quarter), F32)
+    for start in range(0, counts_ref.shape[1], WIDE):
+        cols = slice(start, start + WIDE)
+        numer = numer + cell_block(counts_ref, rows, cols, cells, gene_copy[:, cols])
+    out_ref[:, :quarter] = numer
+    out_ref[:, quarter:] = sums[...]
+
+
+def cell_begin(info, counts, to, cell_turned, mine):
+    n_cells, n_genes = counts.shape
+    return pass_call(
+        functools.partial(cell_begin_kernel, to),
+        info,
+        (counts, cell_turned, mine),
+        struct((RANK, n_cells // X)),
+        n_cells // X,
+        n_genes // CORES,
+        [pltpu.VMEM((GROUPS, 8, n_genes // CORES), F32)],
+    )
 
 
 def cell_quarter(info, counts, to, cell_turned, left, first):
@@ -167,14 +204,14 @@
     quarter = n_cells // X
     sums = struct((RANK, quarter + LANES))
     made = [struct((RANK, n_genes), BF16), struct((RANK, LANES))]
-    return kernel_call(
-        functools.partial(cell_first_kernel if first else cell_block, to),
+    return pass_call(
+        functools.partial(cell_first_kernel if first else cell_later_kernel, to),
         info,
         (counts, cell_turned, *left),
         [sums] + made if first else [sums],
+        quarter,
+        n_genes,
         [pltpu.VMEM((GROUPS, 8, n_genes), F32)] if first else [],
-        vmem=PASS_VMEM,
-        cost=pass_cost(quarter, n_genes),
     )
 
 
@@ -253,6 +290,14 @@
             begun = pass_call(
                 gene_own_kernel, info, (counts, cells[0], gene_copy), struct((RANK, n_genes)), quarter, n_genes
             )
+        begun = pass_call(
+            gene_next_kernel,
+            info,
+            (counts, cells[X - 1], gene_copy, begun),
+            struct((RANK, n_genes)),
+            quarter,
+            n_genes,
+        )
         sent, cell_turned, own = gene_pass(info, counts, begun, gene_copy, cells)
         got = shift(sent, "core", CORES, 1)
         kept = own()
@@ -263,7 +308,7 @@
         mine = swap(spread)
         other = shift(mine, "core", CORES, 1)
 
-        left = (mine, other)
+        left = (cell_begin(info, counts, 2, cell_turned, mine), mine, other)
         got = {}
         for s in (2, 1, 3, 0):
             sums, *made = cell_quarter(info, counts, s, cell_turned, left, not got)

time: 220 us -> 219 us (level)
  waiting for transfers between devices: 37.5 us -> 30.7 us
  Pallas kernels: 49.2 us -> 53 us
    ppermute x27, waiting for transfers between devices: 37.5 us -> 30.7 us  [per_device(): lax.ppermute(a, axis, [(i, (i + s) % n) for i in range(n)])]
    pallas_call x35 -> x41, Pallas kernels: 49.2 us -> 53 us  [kernel_call(): pl.pallas_call(kernel, grid_spec=pltpu.PrefetchScalarGridSpec(num_scalar_...]
  transfers between devices with their start and end apart: 27 -> 27, of which waited for: 15 -> 16; matrix products, arithmetic and copies ran while one was open for 0% -> 0% of each run, Pallas kernels for 7% -> 10%
where the time goes in v1:
time: 219 us; the launch traced here: 214 us
  blocking collectives  77.5 us (35%)
  Pallas kernels  53 us (24%)
  starting transfers between devices  46.8 us (21%)
  waiting for transfers between devices  30.7 us (14%)
  local copies, waits for them, and re-layouts  5.3 us (2%)
    all_to_all x6, blocking collectives, per_device(): swap = lambda a: lax.all_to_all(a, ('y', 'z'), 0, 0, tiled=True)  77.5 us
    pallas_call x41, Pallas kernels, kernel_call(): pl.pallas_call(kernel, grid_spec=pltpu.PrefetchScalarGridSpec(num_scalar_...  53 us
    ppermute x27, starting transfers between devices, per_device(): lax.ppermute(a, axis, [(i, (i + s) % n) for i in range(n)])  46.8 us
    ppermute x27, waiting for transfers between devices, per_device(): lax.ppermute(a, axis, [(i, (i + s) % n) for i in range(n)])  30.7 us
    unnamed x8, local copies, waits for them, and re-layouts  5.3 us
  transfers between devices with their start and end apart: 27, of which 16 were waited for; matrix products, arithmetic and copies ran while one was open for 0% of the time, Pallas kernels for 10%

profile of v1, /device:TPU:8, one launch (start us, length us, event | category | flops | bytes accessed | tf_op | source)
XLA Modules:
  0.0 214.4 jit_solution(6983392752897276635)
XLA Ops:
  0.7 3.4 %copy-done = bf16[2048,2048]{1,0:T(8,128)(2,1)S(1)} copy-done((bf16[2048,2048]{1,0:T(8,128)(2,1)S(1)}, bf16[2048,2048]{1,0:T(8,128)(2,1)}, u32[]{:S(2)}) %copy-start) | copy-done | bytes 8388632
  4.1 0.9 copy-done.1
  5.0 0.9 copy-done.3
  6.0 1.6 shard_map.50
  7.6 1.6 shard_map.51.begun_ref
  9.3 1.7 shard_map.52
  11.1 1.6 shard_map.53.a_ref
  13.2 16.8 %all_to_all.30.parts_ref = f32[16,8,384]{2,1,0:T(8,128)S(1)} all-to-all(f32[16,8,384]{2,1,0:T(8,128)S(1)} %shard_map.54), channel_id=1, replica_groups=mesh['z'=4,'y'=4,'core'=2,'z_hi'=2,'x'=4] {'y','z'}, dimensions={0} | all-to-all | bytes 393216 | tf_op jit(solution)/shard_map/all_to_all | solution.py:276
  30.7 12.1 %all_to_all.31.mine_ref = f32[16,8,256]{2,1,0:T(8,128)S(1)} all-to-all(f32[16,8,256]{2,1,0:T(8,128)S(1)} %get-tuple-element.67), channel_id=1, replica_groups=mesh['z'=4,'y'=4,'core'=2,'z_hi'=2,'x'=4] {'y','z'}, dimensions={0} | all-to-all | bytes 262144 | tf_op jit(solution)/shard_map/all_to_all | solution.py:276
  42.8 1.2 shard_map.56.begun_ref
  44.1 1.2 shard_map.57
  45.3 1.8 shard_map.58
  47.1 1.8 shard_map.59
  48.9 2.8 %collective-permute-start.4 = (f32[32,640]{1,0:T(8,128)S(1)}, f32[32,640]{1,0:T(8,128)S(1)}, u32[]{:S(2)}, u32[]{:S(2)}) collective-permute-start(f32[32,640]{1,0:T(8,128)S(1)} %shard_map.59), channel_id=1, source_target_pairs={{0,3},{1,0},{2,1},{3,2},{4,7},{5,4},{6,5},{7,6},{8,11},{9,8},{10,9... | collective-permute-start | bytes 245768 | tf_op jit(solution)/shard_map/ppermute | solution.py:277
  51.7 2.3 %collective-permute-start.3 = (f32[32,640]{1,0:T(8,128)S(1)}, f32[32,640]{1,0:T(8,128)S(1)}, u32[]{:S(2)}, u32[]{:S(2)}) collective-permute-start(f32[32,640]{1,0:T(8,128)S(1)} %get-tuple-element.76), channel_id=1, source_target_pairs={{0,2},{1,3},{2,0},{3,1},{4,6},{5,7},{6,4},{7,5},{8,10},{9,11},{10,... | collective-permute-start | bytes 245768 | tf_op jit(solution)/shard_map/ppermute | solution.py:277
  54.0 1.8 shard_map.60.a_ref
  55.8 3.3 %collective-permute-done.2.b_ref = f32[32,640]{1,0:T(8,128)S(1)} collective-permute-done((f32[32,640]{1,0:T(8,128)S(1)}, f32[32,640]{1,0:T(8,128)S(1)}, u32[]{:S(2)}, u32[]{:S(2)}) %collective-permute-start.2) | collective-permute-done | bytes 81952 | tf_op jit(solution)/shard_map/ppermute | solution.py:277
  59.7 4.6 %collective-permute-start.5 = (f32[32,640]{1,0:T(8,128)S(1)}, f32[32,640]{1,0:T(8,128)S(1)}, u32[]{:S(2)}, u32[]{:S(2)}) collective-permute-start(f32[32,640]{1,0:T(8,128)S(1)} %shard_map.61.refs_0_), channel_id=1, source_target_pairs={{0,4},{4,0},{1,5},{5,1},{2,6},{6,2},{3,7},{7,3},{8,12},{12,8},{9,1... | collective-permute-start | bytes 245768 | tf_op jit(solution)/shard_map/ppermute | solution.py:277
  64.3 3.9 %collective-permute-done.5.refs_1_ = f32[32,640]{1,0:T(8,128)S(1)} collective-permute-done((f32[32,640]{1,0:T(8,128)S(1)}, f32[32,640]{1,0:T(8,128)S(1)}, u32[]{:S(2)}, u32[]{:S(2)}) %collective-permute-start.5) | collective-permute-done | bytes 81952 | tf_op jit(solution)/shard_map/ppermute | solution.py:277
  68.8 2.6 %collective-permute-start.6 = (f32[32,512]{1,0:T(8,128)S(1)}, f32[32,512]{1,0:T(8,128)S(1)}, u32[]{:S(2)}, u32[]{:S(2)}) collective-permute-start(f32[32,512]{1,0:T(8,128)S(1)} %shard_map.62.piece_ref.f0.old_ref), channel_id=1, source_target_pairs={{0,3},{1,0},{2,1},{3,2},{4,7},{5,4},{6,5},{7,6},{8,11},{9,8},{10,9... | collective-permute-start | bytes 196616 | tf_op jit(solution)/shard_map/ppermute | solution.py:277
  71.6 1.0 collective-permute-start.7
  72.6 1.6 shard_map.63.begun_ref
  74.2 1.6 shard_map.64.begun_ref
  75.8 1.6 collective-permute-done.8.f2
  77.9 1.7 shard_map.65
  79.6 1.6 shard_map.66.a_ref
  81.8 12.0 %all_to_all.32.parts_ref = f32[16,8,384]{2,1,0:T(8,128)S(1)} all-to-all(f32[16,8,384]{2,1,0:T(8,128)S(1)} %shard_map.67), channel_id=1, replica_groups=mesh['z'=4,'y'=4,'core'=2,'z_hi'=2,'x'=4] {'y','z'}, dimensions={0} | all-to-all | bytes 393216 | tf_op jit(solution)/shard_map/all_to_all | solution.py:276
  94.4 12.3 %all_to_all.33.mine_ref = f32[16,8,256]{2,1,0:T(8,128)S(1)} all-to-all(f32[16,8,256]{2,1,0:T(8,128)S(1)} %get-tuple-element.84), channel_id=1, replica_groups=mesh['z'=4,'y'=4,'core'=2,'z_hi'=2,'x'=4] {'y','z'}, dimensions={0} | all-to-all | bytes 262144 | tf_op jit(solution)/shard_map/all_to_all | solution.py:276
  106.7 1.2 shard_map.69.begun_ref
  108.1 1.2 shard_map.70
  109.3 1.8 shard_map.71
  111.1 1.8 shard_map.72
  112.9 0.9 collective-permute-start.13
  113.8 1.1 collective-permute-start.11
  114.9 1.5 collective-permute-start.12
  116.5 1.8 shard_map.73.a_ref
  118.2 3.0 %collective-permute-done.11.b_ref = f32[32,640]{1,0:T(8,128)S(1)} collective-permute-done((f32[32,640]{1,0:T(8,128)S(1)}, f32[32,640]{1,0:T(8,128)S(1)}, u32[]{:S(2)}, u32[]{:S(2)}) %collective-permute-start.11) | collective-permute-done | bytes 81952 | tf_op jit(solution)/shard_map/ppermute | solution.py:277
  121.8 5.0 %collective-permute-start.14 = (f32[32,640]{1,0:T(8,128)S(1)}, f32[32,640]{1,0:T(8,128)S(1)}, u32[]{:S(2)}, u32[]{:S(2)}) collective-permute-start(f32[32,640]{1,0:T(8,128)S(1)} %shard_map.74.refs_0_), channel_id=1, source_target_pairs={{0,4},{4,0},{1,5},{5,1},{2,6},{6,2},{3,7},{7,3},{8,12},{12,8},{9,1... | collective-permute-start | bytes 245768 | tf_op jit(solution)/shard_map/ppermute | solution.py:277
  126.8 4.4 %collective-permute-done.14.refs_1_ = f32[32,640]{1,0:T(8,128)S(1)} collective-permute-done((f32[32,640]{1,0:T(8,128)S(1)}, f32[32,640]{1,0:T(8,128)S(1)}, u32[]{:S(2)}, u32[]{:S(2)}) %collective-permute-start.14) | collective-permute-done | bytes 81952 | tf_op jit(solution)/shard_map/ppermute | solution.py:277
  131.7 11.9 %collective-permute-start.15 = (f32[32,512]{1,0:T(8,128)S(1)}, f32[32,512]{1,0:T(8,128)S(1)}, u32[]{:S(2)}, u32[]{:S(2)}) collective-permute-start(f32[32,512]{1,0:T(8,128)S(1)} %shard_map.75.piece_ref.f0.old_ref), channel_id=1, source_target_pairs={{0,3},{1,0},{2,1},{3,2},{4,7},{5,4},{6,5},{7,6},{8,11},{9,8},{10,9... | collective-permute-start | bytes 196616 | tf_op jit(solution)/shard_map/ppermute | solution.py:277
  143.8 0.9 collective-permute-start.16
  144.7 1.6 shard_map.76.begun_ref
  146.3 1.6 shard_map.77.begun_ref
  148.0 1.5 collective-permute-done.17.f2
  150.0 1.7 shard_map.78
  151.8 1.6 shard_map.79.a_ref
  153.9 12.0 %all_to_all.34.parts_ref = f32[16,8,384]{2,1,0:T(8,128)S(1)} all-to-all(f32[16,8,384]{2,1,0:T(8,128)S(1)} %shard_map.80), channel_id=1, replica_groups=mesh['z'=4,'y'=4,'core'=2,'z_hi'=2,'x'=4] {'y','z'}, dimensions={0} | all-to-all | bytes 393216 | tf_op jit(solution)/shard_map/all_to_all | solution.py:276
  165.9 1.2 shard_map.81
  167.1 12.3 %all_to_all.35.mine_ref = f32[16,8,256]{2,1,0:T(8,128)S(1)} all-to-all(f32[16,8,256]{2,1,0:T(8,128)S(1)} %get-tuple-element.101), channel_id=1, replica_groups=mesh['z'=4,'y'=4,'core'=2,'z_hi'=2,'x'=4] {'y','z'}, dimensions={0} | all-to-all | bytes 262144 | tf_op jit(solution)/shard_map/all_to_all | solution.py:276
  179.5 1.2 shard_map.82.begun_ref
  180.8 1.2 shard_map.83
  182.0 1.8 shard_map.84
  183.8 1.8 shard_map.85
  185.6 1.5 collective-permute-start.22
  187.7 1.4 collective-permute-start.21
  189.1 1.8 shard_map.86.a_ref
  190.9 3.6 %collective-permute-done.20.b_ref = f32[32,640]{1,0:T(8,128)S(1)} collective-permute-done((f32[32,640]{1,0:T(8,128)S(1)}, f32[32,640]{1,0:T(8,128)S(1)}, u32[]{:S(2)}, u32[]{:S(2)}) %collective-permute-start.20) | collective-permute-done | bytes 81952 | tf_op jit(solution)/shard_map/ppermute | solution.py:277
  195.1 4.6 %collective-permute-start.23 = (f32[32,640]{1,0:T(8,128)S(1)}, f32[32,640]{1,0:T(8,128)S(1)}, u32[]{:S(2)}, u32[]{:S(2)}) collective-permute-start(f32[32,640]{1,0:T(8,128)S(1)} %shard_map.87.refs_0_), channel_id=1, source_target_pairs={{0,4},{4,0},{1,5},{5,1},{2,6},{6,2},{3,7},{7,3},{8,12},{12,8},{9,1... | collective-permute-start | bytes 245768 | tf_op jit(solution)/shard_map/ppermute | solution.py:277
  199.7 3.9 %collective-permute-done.23.refs_1_ = f32[32,640]{1,0:T(8,128)S(1)} collective-permute-done((f32[32,640]{1,0:T(8,128)S(1)}, f32[32,640]{1,0:T(8,128)S(1)}, u32[]{:S(2)}, u32[]{:S(2)}) %collective-permute-start.23) | collective-permute-done | bytes 81952 | tf_op jit(solution)/shard_map/ppermute | solution.py:277
  204.2 2.6 %collective-permute-start.26 = (f32[32,512]{1,0:T(8,128)S(1)}, f32[32,512]{1,0:T(8,128)S(1)}, u32[]{:S(2)}, u32[]{:S(2)}) collective-permute-start(f32[32,512]{1,0:T(8,128)S(1)} %shard_map.88.refs_0_), channel_id=1, source_target_pairs={{0,3},{1,0},{2,1},{3,2},{4,7},{5,4},{6,5},{7,6},{8,11},{9,8},{10,9... | collective-permute-start | bytes 196616 | tf_op jit(solution)/shard_map/ppermute | solution.py:277
  206.8 1.0 collective-permute-start.24
  207.8 1.3 shard_map.90
  209.3 3.4 %collective-permute-done.25.refs_2_ = f32[32,512]{1,0:T(8,128)S(1)} collective-permute-done((f32[32,512]{1,0:T(8,128)S(1)}, f32[32,512]{1,0:T(8,128)S(1)}, u32[]{:S(2)}, u32[]{:S(2)}) %collective-permute-start.25) | collective-permute-done | bytes 65568 | tf_op jit(solution)/shard_map/ppermute | solution.py:277
  213.0 1.3 shard_map.89
  (46 shorter events, 9.9 us)
Async XLA Ops:
  0.7 3.4 %copy-start = (bf16[2048,2048]{1,0:T(8,128)(2,1)S(1)}, bf16[2048,2048]{1,0:T(8,128)(2,1)}, u32[]{:S(2)}) copy-start(bf16[2048,2048]{1,0:T(8,128)(2,1)} %counts_ref.53) | copy-start | bytes 25165828
  4.1 0.9 copy-start.1
  5.0 0.9 copy-start.3
  9.3 20.8 %copy-start.2 = (f32[32,2048]{1,0:T(8,128)S(1)}, f32[32,2048]{1,0:T(8,128)}, u32[]{:S(2)}) copy-start(f32[32,2048]{1,0:T(8,128)} %param.5) | copy-start | bytes 786436
  11.0 1.6 collective-permute-start
  42.8 1.3 collective-permute-start.1
  48.9 6.9 %collective-permute-start.4 = (f32[32,640]{1,0:T(8,128)S(1)}, f32[32,640]{1,0:T(8,128)S(1)}, u32[]{:S(2)}, u32[]{:S(2)}) collective-permute-start(f32[32,640]{1,0:T(8,128)S(1)} %shard_map.59), channel_id=1, source_target_pairs={{0,3},{1,0},{2,1},{3,2},{4,7},{5,4},{6,5},{7,6},{8,11},{9,8},{10,9... | collective-permute-start | bytes 245768 | tf_op jit(solution)/shard_map/ppermute | solution.py:277
  51.7 7.4 %collective-permute-start.2 = (f32[32,640]{1,0:T(8,128)S(1)}, f32[32,640]{1,0:T(8,128)S(1)}, u32[]{:S(2)}, u32[]{:S(2)}) collective-permute-start(f32[32,640]{1,0:T(8,128)S(1)} %shard_map.58), channel_id=1, source_target_pairs={{0,1},{1,2},{2,3},{3,0},{4,5},{5,6},{6,7},{7,4},{8,9},{9,10},{10,1... | collective-permute-start | bytes 245768 | tf_op jit(solution)/shard_map/ppermute | solution.py:277
  51.7 7.4 %collective-permute-start.3 = (f32[32,640]{1,0:T(8,128)S(1)}, f32[32,640]{1,0:T(8,128)S(1)}, u32[]{:S(2)}, u32[]{:S(2)}) collective-permute-start(f32[32,640]{1,0:T(8,128)S(1)} %get-tuple-element.76), channel_id=1, source_target_pairs={{0,2},{1,3},{2,0},{3,1},{4,6},{5,7},{6,4},{7,5},{8,10},{9,11},{10,... | collective-permute-start | bytes 245768 | tf_op jit(solution)/shard_map/ppermute | solution.py:277
  59.7 8.5 %collective-permute-start.5 = (f32[32,640]{1,0:T(8,128)S(1)}, f32[32,640]{1,0:T(8,128)S(1)}, u32[]{:S(2)}, u32[]{:S(2)}) collective-permute-start(f32[32,640]{1,0:T(8,128)S(1)} %shard_map.61.refs_0_), channel_id=1, source_target_pairs={{0,4},{4,0},{1,5},{5,1},{2,6},{6,2},{3,7},{7,3},{8,12},{12,8},{9,1... | collective-permute-start | bytes 245768 | tf_op jit(solution)/shard_map/ppermute | solution.py:277
  68.8 5.4 %collective-permute-start.6 = (f32[32,512]{1,0:T(8,128)S(1)}, f32[32,512]{1,0:T(8,128)S(1)}, u32[]{:S(2)}, u32[]{:S(2)}) collective-permute-start(f32[32,512]{1,0:T(8,128)S(1)} %shard_map.62.piece_ref.f0.old_ref), channel_id=1, source_target_pairs={{0,3},{1,0},{2,1},{3,2},{4,7},{5,4},{6,5},{7,6},{8,11},{9,8},{10,9... | collective-permute-start | bytes 196616 | tf_op jit(solution)/shard_map/ppermute | solution.py:277
  71.4 6.1 %collective-permute-start.8 = (f32[32,512]{1,0:T(8,128)S(1)}, f32[32,512]{1,0:T(8,128)S(1)}, u32[]{:S(2)}, u32[]{:S(2)}) collective-permute-start(f32[32,512]{1,0:T(8,128)S(1)} %shard_map.62.piece_ref.f0.old_ref), channel_id=1, source_target_pairs={{0,2},{1,3},{2,0},{3,1},{4,6},{5,7},{6,4},{7,5},{8,10},{9,11},{10,... | collective-permute-start | bytes 196616 | tf_op jit(solution)/shard_map/ppermute | solution.py:277
  71.6 6.3 %collective-permute-start.7 = (f32[32,512]{1,0:T(8,128)S(1)}, f32[32,512]{1,0:T(8,128)S(1)}, u32[]{:S(2)}, u32[]{:S(2)}) collective-permute-start(f32[32,512]{1,0:T(8,128)S(1)} %shard_map.62.piece_ref.f0.old_ref), channel_id=1, source_target_pairs={{0,1},{1,2},{2,3},{3,0},{4,5},{5,6},{6,7},{7,4},{8,9},{9,10},{10,1... | collective-permute-start | bytes 196616 | tf_op jit(solution)/shard_map/ppermute | solution.py:277
  79.6 1.6 collective-permute-start.9
  106.7 1.3 collective-permute-start.10
  112.9 5.4 %collective-permute-start.13 = (f32[32,640]{1,0:T(8,128)S(1)}, f32[32,640]{1,0:T(8,128)S(1)}, u32[]{:S(2)}, u32[]{:S(2)}) collective-permute-start(f32[32,640]{1,0:T(8,128)S(1)} %shard_map.72), channel_id=1, source_target_pairs={{0,3},{1,0},{2,1},{3,2},{4,7},{5,4},{6,5},{7,6},{8,11},{9,8},{10,9... | collective-permute-start | bytes 245768 | tf_op jit(solution)/shard_map/ppermute | solution.py:277
  113.8 7.4 %collective-permute-start.11 = (f32[32,640]{1,0:T(8,128)S(1)}, f32[32,640]{1,0:T(8,128)S(1)}, u32[]{:S(2)}, u32[]{:S(2)}) collective-permute-start(f32[32,640]{1,0:T(8,128)S(1)} %shard_map.71), channel_id=1, source_target_pairs={{0,1},{1,2},{2,3},{3,0},{4,5},{5,6},{6,7},{7,4},{8,9},{9,10},{10,1... | collective-permute-start | bytes 245768 | tf_op jit(solution)/shard_map/ppermute | solution.py:277
  114.9 6.3 %collective-permute-start.12 = (f32[32,640]{1,0:T(8,128)S(1)}, f32[32,640]{1,0:T(8,128)S(1)}, u32[]{:S(2)}, u32[]{:S(2)}) collective-permute-start(f32[32,640]{1,0:T(8,128)S(1)} %get-tuple-element.93), channel_id=1, source_target_pairs={{0,2},{1,3},{2,0},{3,1},{4,6},{5,7},{6,4},{7,5},{8,10},{9,11},{10,... | collective-permute-start | bytes 245768 | tf_op jit(solution)/shard_map/ppermute | solution.py:277
  121.8 9.3 %collective-permute-start.14 = (f32[32,640]{1,0:T(8,128)S(1)}, f32[32,640]{1,0:T(8,128)S(1)}, u32[]{:S(2)}, u32[]{:S(2)}) collective-permute-start(f32[32,640]{1,0:T(8,128)S(1)} %shard_map.74.refs_0_), channel_id=1, source_target_pairs={{0,4},{4,0},{1,5},{5,1},{2,6},{6,2},{3,7},{7,3},{8,12},{12,8},{9,1... | collective-permute-start | bytes 245768 | tf_op jit(solution)/shard_map/ppermute | solution.py:277
  131.7 14.6 %collective-permute-start.15 = (f32[32,512]{1,0:T(8,128)S(1)}, f32[32,512]{1,0:T(8,128)S(1)}, u32[]{:S(2)}, u32[]{:S(2)}) collective-permute-start(f32[32,512]{1,0:T(8,128)S(1)} %shard_map.75.piece_ref.f0.old_ref), channel_id=1, source_target_pairs={{0,3},{1,0},{2,1},{3,2},{4,7},{5,4},{6,5},{7,6},{8,11},{9,8},{10,9... | collective-permute-start | bytes 196616 | tf_op jit(solution)/shard_map/ppermute | solution.py:277
  143.6 5.9 %collective-permute-start.17 = (f32[32,512]{1,0:T(8,128)S(1)}, f32[32,512]{1,0:T(8,128)S(1)}, u32[]{:S(2)}, u32[]{:S(2)}) collective-permute-start(f32[32,512]{1,0:T(8,128)S(1)} %shard_map.75.piece_ref.f0.old_ref), channel_id=1, source_target_pairs={{0,2},{1,3},{2,0},{3,1},{4,6},{5,7},{6,4},{7,5},{8,10},{9,11},{10,... | collective-permute-start | bytes 196616 | tf_op jit(solution)/shard_map/ppermute | solution.py:277
  143.8 6.2 %collective-permute-start.16 = (f32[32,512]{1,0:T(8,128)S(1)}, f32[32,512]{1,0:T(8,128)S(1)}, u32[]{:S(2)}, u32[]{:S(2)}) collective-permute-start(f32[32,512]{1,0:T(8,128)S(1)} %shard_map.75.piece_ref.f0.old_ref), channel_id=1, source_target_pairs={{0,1},{1,2},{2,3},{3,0},{4,5},{5,6},{6,7},{7,4},{8,9},{9,10},{10,1... | collective-permute-start | bytes 196616 | tf_op jit(solution)/shard_map/ppermute | solution.py:277
  151.7 1.7 collective-permute-start.18
  179.5 1.3 collective-permute-start.19
  185.6 5.3 %collective-permute-start.22 = (f32[32,640]{1,0:T(8,128)S(1)}, f32[32,640]{1,0:T(8,128)S(1)}, u32[]{:S(2)}, u32[]{:S(2)}) collective-permute-start(f32[32,640]{1,0:T(8,128)S(1)} %shard_map.85), channel_id=1, source_target_pairs={{0,3},{1,0},{2,1},{3,2},{4,7},{5,4},{6,5},{7,6},{8,11},{9,8},{10,9... | collective-permute-start | bytes 245768 | tf_op jit(solution)/shard_map/ppermute | solution.py:277
  187.1 7.4 %collective-permute-start.20 = (f32[32,640]{1,0:T(8,128)S(1)}, f32[32,640]{1,0:T(8,128)S(1)}, u32[]{:S(2)}, u32[]{:S(2)}) collective-permute-start(f32[32,640]{1,0:T(8,128)S(1)} %shard_map.84), channel_id=1, source_target_pairs={{0,1},{1,2},{2,3},{3,0},{4,5},{5,6},{6,7},{7,4},{8,9},{9,10},{10,1... | collective-permute-start | bytes 245768 | tf_op jit(solution)/shard_map/ppermute | solution.py:277
  187.7 6.8 %collective-permute-start.21 = (f32[32,640]{1,0:T(8,128)S(1)}, f32[32,640]{1,0:T(8,128)S(1)}, u32[]{:S(2)}, u32[]{:S(2)}) collective-permute-start(f32[32,640]{1,0:T(8,128)S(1)} %get-tuple-element.110), channel_id=1, source_target_pairs={{0,2},{1,3},{2,0},{3,1},{4,6},{5,7},{6,4},{7,5},{8,10},{9,11},{10,... | collective-permute-start | bytes 245768 | tf_op jit(solution)/shard_map/ppermute | solution.py:277
  195.1 8.5 %collective-permute-start.23 = (f32[32,640]{1,0:T(8,128)S(1)}, f32[32,640]{1,0:T(8,128)S(1)}, u32[]{:S(2)}, u32[]{:S(2)}) collective-permute-start(f32[32,640]{1,0:T(8,128)S(1)} %shard_map.87.refs_0_), channel_id=1, source_target_pairs={{0,4},{4,0},{1,5},{5,1},{2,6},{6,2},{3,7},{7,3},{8,12},{12,8},{9,1... | collective-permute-start | bytes 245768 | tf_op jit(solution)/shard_map/ppermute | solution.py:277
  204.2 5.1 %collective-permute-start.26 = (f32[32,512]{1,0:T(8,128)S(1)}, f32[32,512]{1,0:T(8,128)S(1)}, u32[]{:S(2)}, u32[]{:S(2)}) collective-permute-start(f32[32,512]{1,0:T(8,128)S(1)} %shard_map.88.refs_0_), channel_id=1, source_target_pairs={{0,3},{1,0},{2,1},{3,2},{4,7},{5,4},{6,5},{7,6},{8,11},{9,8},{10,9... | collective-permute-start | bytes 196616 | tf_op jit(solution)/shard_map/ppermute | solution.py:277
  206.8 5.9 %collective-permute-start.25 = (f32[32,512]{1,0:T(8,128)S(1)}, f32[32,512]{1,0:T(8,128)S(1)}, u32[]{:S(2)}, u32[]{:S(2)}) collective-permute-start(f32[32,512]{1,0:T(8,128)S(1)} %shard_map.88.refs_0_), channel_id=1, source_target_pairs={{0,2},{1,3},{2,0},{3,1},{4,6},{5,7},{6,4},{7,5},{8,10},{9,11},{10,... | collective-permute-start | bytes 196616 | tf_op jit(solution)/shard_map/ppermute | solution.py:277
  206.8 6.2 %collective-permute-start.24 = (f32[32,512]{1,0:T(8,128)S(1)}, f32[32,512]{1,0:T(8,128)S(1)}, u32[]{:S(2)}, u32[]{:S(2)}) collective-permute-start(f32[32,512]{1,0:T(8,128)S(1)} %shard_map.88.refs_0_), channel_id=1, source_target_pairs={{0,1},{1,2},{2,3},{3,0},{4,5},{5,6},{6,7},{7,4},{8,9},{9,10},{10,1... | collective-permute-start | bytes 196616 | tf_op jit(solution)/shard_map/ppermute | solution.py:277
